TPU v7x, 32 devices: a whole 2x2x4 slice. The times are simulated.
32 devices in a mesh: space: 16 (over z, y, core), mem: 2 (over x).
Axes of the slice: x: 2, y: 2, z: 4, core: 2. Of those that a mesh axis runs over, the one named last changes fastest.
Arguments:
- member_heat_solute: float32 [128, 2, 256, 128], P('mem', None, 'space'), may hold values from -6 to 6
- velocity: float32 [128, 256, 128], P('mem', 'space'), may hold values from 0.2 to 0.6
- phase_mask: int32 [256, 128], P('space'), may hold values 0 or 1
- obs_index: int32 [256], P('space'), may hold values from 0 to 2047
- obs_value: float32 [256], P('space'), may hold values from -6 to 6
- obs_error: float32 [256], P('space'), may hold values from 0.3 to 3
Outputs:
- analysis_hc: float32 [128, 2, 256, 128], P('mem', None, 'space')
- analysis_velocity: float32 [128, 256, 128], P('mem', 'space')
Inputs may be any that keep to these rules, and one draw needn't show every extreme that they name: `obs_index`: observation o lies in slab o // 16; its entry counts cells row by row inside that slab.
All inputs are finite; a program needn't handle non-finite values. No bound on the sum of `phase_mask` on one device may be relied on, other than what follows from the above.
Results may differ from a plain program's by a relative error of at most 0.00015.
Values sent between devices are 32-bit elements; how exact they have to be, the bound alone decides.
A program may use at most 64 MiB of HBM per device.

v0:
```python
import jax
import jax.numpy as jnp
from jax import lax
from jax.sharding import PartitionSpec as P

heat_diffusion = 0.15
advection = 0.4
solute_diffusion = 0.05
segregation = 0.3
momentum_diffusion = 0.1
darcy_drag = 0.5
mushy_ratio = 1.0 / 3.0


def with_halo(cells, sides, width):
    for axis, dim in sides:
        count = lax.axis_size(axis)
        ends = count - 1
        head = lax.slice_in_dim(cells, 0, width, axis=dim)
        tail = lax.slice_in_dim(cells, cells.shape[dim] - width, cells.shape[dim], axis=dim)
        cells = jnp.concatenate(
            [
                lax.ppermute(tail, axis, [(i, (i + 1) % count) for i in range(ends)]),
                cells,
                lax.ppermute(head, axis, [((i + 1) % count, i) for i in range(ends)]),
            ],
            axis=dim,
        )
    return cells


def lateral(field):
    left = jnp.concatenate([field[..., :1], field[..., :-1]], axis=-1)
    right = jnp.concatenate([field[..., 1:], field[..., -1:]], axis=-1)
    return left + right - 2.0 * field


def advance(padded_heat, padded_temp, padded_solute, padded_speed, mushy):
    heat = padded_heat[..., 1:-1, :]
    temp = padded_temp[..., 1:-1, :]
    solute = padded_solute[..., 1:-1, :]
    speed = padded_speed[..., 1:-1, :]
    temp_lap = padded_temp[..., 2:, :] + padded_temp[..., :-2, :] - 2.0 * temp + lateral(temp)
    solute_lap = (
        padded_solute[..., 2:, :] + padded_solute[..., :-2, :] - 2.0 * solute + lateral(solute)
    )
    speed_lap = padded_speed[..., 2:, :] + padded_speed[..., :-2, :] - 2.0 * speed + lateral(speed)
    new_heat = (
        heat + heat_diffusion * temp_lap - advection * speed * (heat - padded_heat[..., :-2, :])
    )
    new_solute = (
        solute
        + solute_diffusion * solute_lap
        - advection * speed * (solute - padded_solute[..., :-2, :])
        + segregation * mushy * (temp - solute)
    )
    new_speed = speed + momentum_diffusion * speed_lap - darcy_drag * mushy * speed
    return (new_heat, new_solute, new_speed)


def factorize(matrix):
    order = matrix.shape[0]
    positions = jnp.arange(order, dtype=jnp.int32)

    def column(j, lower):
        lower_row = lax.dynamic_slice_in_dim(lower, j, 1, 0)[0]
        matrix_col = lax.dynamic_slice_in_dim(matrix, j, 1, 1)[:, 0]
        values = matrix_col - jnp.dot(lower, lower_row, precision=lax.Precision.HIGHEST)
        pivot = jnp.sqrt(jnp.sum(jnp.where(positions == j, values, 0.0)))
        new_col = jnp.where(positions >= j, values / pivot, 0.0)
        return lax.dynamic_update_slice(lower, new_col[:, None], (jnp.int32(0), j))

    return lax.fori_loop(0, order, column, jnp.zeros((order, order), jnp.float32))


def invert_lower(lower):
    order = lower.shape[0]
    positions = jnp.arange(order, dtype=jnp.int32)

    def row_step(i, inverse):
        lower_row = lax.dynamic_slice_in_dim(lower, i, 1, 0)[0]
        pivot = jnp.sum(jnp.where(positions == i, lower_row, 0.0))
        unit = jnp.where(positions == i, 1.0, 0.0).astype(jnp.float32)
        new_row = (unit - jnp.dot(lower_row, inverse, precision=lax.Precision.HIGHEST)) / pivot
        return lax.dynamic_update_slice(inverse, new_row[None, :], (i, jnp.int32(0)))

    return lax.fori_loop(0, order, row_step, jnp.zeros((order, order), jnp.float32))


def analysis_weights(gram, project):
    members = gram.shape[0]
    ident = jnp.eye(members, dtype=jnp.float32)
    lower = factorize(ident + gram)
    lower_inverse = invert_lower(lower)
    inverse_root = lower_inverse.T
    mean_offset = jnp.dot(
        inverse_root,
        jnp.dot(lower_inverse, project, precision=lax.Precision.HIGHEST),
        precision=lax.Precision.HIGHEST,
    )
    center = ident - 1.0 / members
    combined = mean_offset[:, None] / jnp.sqrt(jnp.float32(members - 1)) + inverse_root
    return 1.0 / members + jnp.dot(center, combined, precision=lax.Precision.HIGHEST)


def on_device(member_heat_solute, velocity, phase_mask, obs_index, obs_value, obs_error):
    members = member_heat_solute.shape[0]
    mushy = phase_mask.astype(jnp.float32)
    factor = 1.0 - mushy * (1.0 - mushy_ratio)
    heat = member_heat_solute[:, 0]
    solute = member_heat_solute[:, 1]
    speed = velocity
    for section in range(2):
        field_stack = jnp.stack([heat, heat * factor, solute, speed], axis=1)
        padded = with_halo(field_stack, (("space", 2),), 1)
        heat, solute, speed = advance(padded[:, 0], padded[:, 1], padded[:, 2], padded[:, 3], mushy)
    temp = heat * factor
    flat_temp = temp.reshape(members, -1)
    cell_ids = jnp.arange(flat_temp.shape[1], dtype=jnp.int32)
    selector = jnp.where(obs_index[:, None] == cell_ids[None, :], 1.0, 0.0).astype(jnp.float32)
    observed_own = jnp.dot(flat_temp, selector.T, precision=lax.Precision.HIGHEST)
    measured_values = lax.all_gather(observed_own, "mem", axis=0, tiled=True)
    ensemble = measured_values.shape[0]
    mean_obs = jnp.mean(measured_values, axis=0)
    spread = (measured_values - mean_obs[None, :]).T / (
        obs_error[:, None] * jnp.sqrt(jnp.float32(ensemble - 1))
    )
    innovation = (obs_value - mean_obs) / obs_error
    local_gram = jnp.dot(spread.T, spread, precision=lax.Precision.HIGHEST)
    local_project = jnp.dot(spread.T, innovation, precision=lax.Precision.HIGHEST)
    gram, project = lax.psum((local_gram, local_project), "space")
    mixing = analysis_weights(gram, project)
    states = jnp.concatenate([heat[:, None], solute[:, None], speed[:, None]], axis=1)
    first_member = lax.axis_index("mem") * members
    weight_cols = lax.dynamic_slice_in_dim(mixing, first_member, members, 1)
    result = jnp.einsum(
        "kfzw,kj->jfzw",
        lax.all_gather(states, "mem", axis=0, tiled=True),
        weight_cols,
        precision=lax.Precision.HIGHEST,
    )
    return (result[:, :2], result[:, 2])


def solution(mesh):
    return jax.shard_map(
        on_device,
        mesh=mesh,
        in_specs=(
            P("mem", None, "space", None),
            P("mem", "space", None),
            P("space", None),
            P("space"),
            P("space"),
            P("space"),
        ),
        out_specs=(P("mem", None, "space", None), P("mem", "space", None)),
        check_vma=False,
    )
```

profile of v0, /device:TPU:0, one launch (start us, length us, event | category | flops | bytes accessed | tf_op | source)
XLA Modules:
  0.0 589.5 jit_solution(1841396071073191098)
XLA Ops:
  8.8 1.3 fusion.84
  10.7 2.4 collective-permute-start
  13.0 1.3 collective-permute-start.1
  14.4 4.1 collective-permute-done.1
  20.4 0.9 multiply_bitcast_fusion.1
  21.4 5.5 collective-permute-start.2
  26.8 1.3 collective-permute-start.3
  28.2 1.9 collective-permute-done.3
  31.6 0.9 fusion.88
  32.6 1.9 multiply_bitcast_fusion
  35.0 4.4 all-gather
  39.6 1.0 fusion.81
  40.7 1.7 fusion.30
  42.4 1.3 pad_maximum_fusion.2
  43.9 32.2 %psum.15 = f32[128]{0:T(128)S(1)} all-reduce(f32[128]{0:T(128)S(1)} %convolution_bitcast_fusion.5), channel_id=1, replica_groups=mesh['space'=16,'mem'=2] {'space'}, use_global_device_ids=true, to_apply=%region_8.9 | all-reduce | flops 128 | bytes 1024 | tf_op jit(solution)/shard_map/psum | solution.py:131
  76.1 52.7 %all-reduce.2.cloned.1.call-done = f32[128,128]{1,0:T(8,128)} async-done(((f32[128,128]{1,0:T(8,128)}), f32[128,128]{1,0:T(8,128)}) %all-reduce.2.cloned.1.call-update) | async-done | bytes 65552 | tf_op jit(solution)/shard_map/psum | solution.py:131
  128.8 0.9 convert_add_fusion
  129.8 258.7 %while.30 = (s32[]{:T(128)}, f32[128,128]{1,0:T(8,128)S(1)}, f32[128,128]{0,1:T(8,128)S(1)}, s32[]{:T(128)}, s32[]{:T(128)}) while((s32[]{:T(128)}, f32[128,128]{1,0:T(8,128)S(1)}, f32[128,128]{0,1:T(8,128)S(1)}, s32[]{:T(128)}, s32[]{:T(128)}) %tuple.105), condition=%wide.region_4.5_spmd.clone.clone, body=%wide.region_2.0_spmd.clone.clone.sunk | while | flops 197505 | bytes 71765 | solution.py:73
  129.8 0.8 fusion.115
  131.7 0.8 fusion.115
  133.7 0.8 fusion.115
  135.8 0.8 fusion.115
  137.8 0.8 fusion.115
  139.8 0.8 fusion.115
  141.8 0.8 fusion.115
  143.8 0.8 fusion.115
  145.9 0.8 fusion.115
  147.9 0.8 fusion.115
  149.9 0.8 fusion.115
  151.9 0.8 fusion.115
  154.0 0.8 fusion.115
  156.0 0.8 fusion.115
  158.0 0.8 fusion.115
  160.0 0.8 fusion.115
  162.0 0.8 fusion.115
  164.1 0.8 fusion.115
  166.1 0.8 fusion.115
  168.1 0.8 fusion.115
  170.1 0.8 fusion.115
  172.2 0.8 fusion.115
  174.2 0.8 fusion.115
  176.2 0.8 fusion.115
  178.2 0.8 fusion.115
  180.2 0.8 fusion.115
  388.5 186.3 %while.29 = (s32[]{:T(128)}, f32[128,128]{1,0:T(8,128)S(1)}, f32[128,128]{1,0:T(8,128)S(1)}, s32[]{:T(128)}, s32[]{:T(128)}) while((s32[]{:T(128)}, f32[128,128]{1,0:T(8,128)S(1)}, f32[128,128]{1,0:T(8,128)S(1)}, s32[]{:T(128)}, s32[]{:T(128)}) %tuple.108), condition=%wide.region_7.8_spmd.clone, body=%wide.region_5.7_spmd.clone.sunk | while | flops 197505 | bytes 70725 | solution.py:87
  575.5 3.7 fusion.69
  579.3 1.6 copy.31
  580.9 1.1 copy.32
  (924 shorter events, 335.2 us)
Async XLA Ops:
  8.0 2.3 copy-start.2
  8.0 120.8 %all-reduce.2.cloned.1.call-start = ((), (), s32[]{:S(2)}) async-start(), calls=%async_computation | async-start | bytes 131072 | tf_op jit(solution)/shard_map/psum | solution.py:131
  10.7 3.7 collective-permute-start
  13.0 5.4 collective-permute-start.1
  21.3 6.8 %copy-start.4 = (f32[16]{0:T(128)S(1)}, f32[16]{0:T(128)}, u32[]{:S(2)}) copy-start(f32[16]{0:T(128)} %param.15) | copy-start | bytes 196
  21.4 6.8 %collective-permute-start.2 = (f32[64,4,1,128]{3,0,2,1:T(8,128)S(1)}, f32[64,4,1,128]{3,0,2,1:T(8,128)S(1)}, u32[]{:S(2)}, u32[]{:S(2)}) collective-permute-start(f32[64,4,1,128]{3,0,2,1:T(8,128)S(1)} %get-tuple-element.234), channel_id=1, source_target_pairs={{0,2},{2,4},{4,6},{6,8},{8,10},{10,12},{12,14},{14,16},{16,18},{18... | collective-permute-start | bytes 393224 | tf_op jit(solution)/shard_map/ppermute | solution.py:23
  26.8 3.2 collective-permute-start.3
  32.6 1.9 copy-start.3
  40.6 534.9 %all-gather.3.cloned.1.call-start = ((), (), s32[]{:S(2)}) async-start(), calls=%async_computation.1 | async-start | bytes 4718592 | tf_op jit(solution)/shard_map/all_gather | solution.py:138
  40.6 1.7 copy-start
  40.7 1.7 copy-start.1
  42.4 1.3 copy-start.5
Sparse Core Ops, SparseCore 0:
  40.7 88.0 all-reduce.1
Sparse Core Ops, SparseCore 1:
  76.2 42.0 all-gather.2
where the time goes:
time: 593 us; the launch traced here: 589 us
  matrix products  213 us (36%)
  loops' own time  95.3 us (16%)
  other arithmetic  87 us (15%)
  local copies, waits for them, and re-layouts  72.6 us (12%)
  waiting for transfers between devices  58.8 us (10%)
  blocking collectives  36.6 us (6%)
  between operations  15.8 us (3%)
  starting transfers between devices  10.5 us (2%)
    dot_general x128, matrix products, column(): jnp.dot(lower, lower_row, precision=lax.Precision.HIGHEST)  105 us
    dot_general x128, matrix products, row_step(): jnp.dot(lower_row, inverse, precision=lax.Precision.HIGHEST)  102 us
    another operation x1, loops' own time, factorize(): lax.fori_loop(0, order, column, jnp.zeros((order, order), jnp.float32))  92.6 us
    reduce_sum x128, other arithmetic, row_step(): pivot = jnp.sum(jnp.where(positions == i, lower_row, 0.0))  77.6 us
    psum x1, waiting for transfers between devices, on_device(): gram, project = lax.psum((local_gram, local_project), 'space')  52.7 us
    dynamic_update_slice x128, local copies, waits for them, and re-layouts, column(): return lax.dynamic_update_slice(lower, new_col[:, None], (jnp.int32(0), j))  45.9 us
    psum x1, blocking collectives, on_device(): gram, project = lax.psum((local_gram, local_project), 'space')  32.2 us
    broadcast_in_dim x128, local copies, waits for them, and re-layouts, column(): return lax.dynamic_update_slice(lower, new_col[:, None], (jnp.int32(0), j))  14.5 us
  transfers between devices with their start and end apart: 6, of which 3 were waited for; matrix products, arithmetic and copies ran while one was open for 60% of the time, Pallas kernels for 0%

commit v1 on v0

v1 whole, which is shorter than its diff:
```python
import functools

import jax
import jax.numpy as jnp
from jax import lax
from jax.experimental import pallas as pl
from jax.experimental.pallas import tpu as pltpu
from jax.sharding import PartitionSpec as P

heat_diffusion = 0.15
advection = 0.4
solute_diffusion = 0.05
segregation = 0.3
momentum_diffusion = 0.1
darcy_drag = 0.5
mushy_ratio = 1.0 / 3.0

MESH = pl.DeviceIdType.MESH
HIGHEST = lax.Precision.HIGHEST
HEAT, SOLUTE, SPEED = 0, 1, 2
PANEL = 8


def lateral_sum(field):
    lane = lax.broadcasted_iota(jnp.int32, field.shape, 2)
    last = field.shape[2] - 1
    left = jnp.where(lane == 0, field, pltpu.roll(field, 1, 2))
    right = jnp.where(lane == last, field, pltpu.roll(field, last, 2))
    return left + right


def laplacian(field):
    centre = field[1:-1]
    return field[2:] + field[:-2] + lateral_sum(centre) - 4.0 * centre


def advance_speed(speed, mushy):
    centre = speed[1:-1]
    return centre + momentum_diffusion * laplacian(speed) - darcy_drag * mushy[1:-1] * centre


def advance_pair(heat, solute, speed, mushy):
    temp = heat * (1.0 - mushy * (1.0 - mushy_ratio))
    drift = advection * speed[1:-1]
    new_heat = (
        heat[1:-1] + heat_diffusion * laplacian(temp) - drift * (heat[1:-1] - heat[:-2])
    )
    new_solute = (
        solute[1:-1]
        + solute_diffusion * laplacian(solute)
        - drift * (solute[1:-1] - solute[:-2])
        + segregation * mushy[1:-1] * (temp[1:-1] - solute[1:-1])
    )
    return new_heat, new_solute


def split(values):
    high = values.astype(jnp.bfloat16)
    low = (values - high.astype(jnp.float32)).astype(jnp.bfloat16)
    return high, low


def inverse_factor(matrix_ref):
    order = matrix_ref.shape[0]
    lane = lax.broadcasted_iota(jnp.int32, (PANEL, order), 1)
    sub = lax.broadcasted_iota(jnp.int32, (PANEL, order), 0)
    rows = lax.broadcasted_iota(jnp.int32, (order, order), 0)
    lanes = lax.broadcasted_iota(jnp.int32, (order, order), 1)

    def panel(block, carry):
        base = pl.multiple_of(block * PANEL, PANEL)
        here = matrix_ref[pl.ds(base, PANEL), :]
        cols = [
            jnp.broadcast_to(
                jnp.sum(jnp.where(lane == base + s, here, 0.0), axis=1, keepdims=True),
                (PANEL, order),
            )
            for s in range(PANEL)
        ]
        upper = jnp.where(lane >= base, here, 0.0)
        inverse = jnp.where(lane < base, here, jnp.where(lane == base + sub, 1.0, 0.0))
        diagonal = jnp.zeros((PANEL, order), jnp.float32)
        for s in range(PANEL):
            pivot = cols[s][s : s + 1]
            diagonal = jnp.where(sub == s, pivot, diagonal)
            factor = jnp.where(sub > s, cols[s] / pivot, 0.0)
            upper = upper - factor * upper[s : s + 1]
            inverse = inverse - factor * inverse[s : s + 1]
            for t in range(s + 1, PANEL):
                cols[t] = cols[t] - factor * cols[t][s : s + 1]
        scale = 1.0 / jnp.sqrt(diagonal)
        upper = upper * scale
        inverse = inverse * scale
        right = jnp.where(lane < base + PANEL, inverse, upper)
        change = lax.dot_general(
            upper, right, (((0,), (0,)), ((), ())),
            precision=HIGHEST, preferred_element_type=jnp.float32,
        )
        old = matrix_ref[...]
        kept = jnp.where((lanes >= base) & (lanes < base + PANEL), 0.0, old)
        matrix_ref[...] = jnp.where(rows >= base + PANEL, kept - change, old)
        matrix_ref[pl.ds(base, PANEL), :] = inverse
        return carry

    lax.fori_loop(0, order // PANEL, panel, 0)


def kernel(
    slabs, halves,
    hc_ref, v_ref, mask_ref, index_ref, value_ref, error_ref,
    out_hc_ref, out_v_ref,
    hc, vel, raw, mushy, own, other, seen, square,
    in_sem, out_sem, halo_send, halo_recv, state_send, state_recv, seen_send, seen_recv,
):
    members = own.shape[2]
    width = own.shape[3]
    depth = own.shape[1]
    groups = members // 8
    everyone = slabs * halves
    ens = members * halves
    slab = lax.axis_index("space")
    half = lax.axis_index("mem")
    me = slab * halves + half
    first = slab == 0
    last = slab == slabs - 1

    load_v = pltpu.make_async_copy(v_ref, vel, in_sem.at[0])
    load_hc = pltpu.make_async_copy(hc_ref, hc, in_sem.at[1])
    load_v.start()
    load_hc.start()

    barrier = pltpu.get_barrier_semaphore()

    def greet(step, carry):
        peer = lax.rem(me + step, everyone)
        pl.semaphore_signal(
            barrier, inc=1, device_id=(peer // halves, lax.rem(peer, halves)), device_id_type=MESH
        )
        return carry

    lax.fori_loop(1, everyone, greet, 0)

    for z in range(depth):
        row = mask_ref[z : z + 1, :].astype(jnp.float32)
        mushy[z + 2] = jnp.broadcast_to(row, (8, width))

    def relayout(zs):
        for z in zs:
            raw[HEAT, z + 2] = hc[pl.ds(z, members, stride=2 * depth), :]
            raw[SOLUTE, z + 2] = hc[pl.ds(depth + z, members, stride=2 * depth), :]
            raw[SPEED, z + 2] = vel[pl.ds(z, members, stride=depth), :]

    load_v.wait()
    load_hc.wait()
    relayout((0, 1, depth - 2, depth - 1))

    def halo(direction, source, target, to, part):
        ref = raw if part == 0 else mushy
        pick = (lambda r, a: r.at[:, pl.ds(a, 2)]) if part == 0 else (lambda r, a: r.at[pl.ds(a, 2)])
        return pltpu.make_async_remote_copy(
            src_ref=pick(ref, source),
            dst_ref=pick(ref, target),
            send_sem=halo_send.at[direction, part],
            recv_sem=halo_recv.at[direction, part],
            device_id=(to, half),
            device_id_type=MESH,
        )

    up = [halo(0, 2, depth + 2, lax.rem(slab + slabs - 1, slabs), part) for part in range(2)]
    down = [halo(1, depth, 0, lax.rem(slab + 1, slabs), part) for part in range(2)]

    @pl.when(first)
    def _():
        raw[:, 0:2] = jnp.zeros((3, 2, members, width), jnp.float32)
        mushy[0:2] = jnp.zeros((2, 8, width), jnp.float32)

    @pl.when(last)
    def _():
        raw[:, depth + 2 : depth + 4] = jnp.zeros((3, 2, members, width), jnp.float32)
        mushy[depth + 2 : depth + 4] = jnp.zeros((2, 8, width), jnp.float32)

    pl.semaphore_wait(barrier, everyone - 1)

    @pl.when(jnp.logical_not(first))
    def _():
        for copy in up:
            copy.start()

    @pl.when(jnp.logical_not(last))
    def _():
        for copy in down:
            copy.start()

    relayout(range(2, depth - 2))

    pieces = []

    def send(field, start, count):
        number = len(pieces)
        copies = []
        for hop in range(1, halves):
            copies.append(
                pltpu.make_async_remote_copy(
                    src_ref=own.at[field, pl.ds(start, count)],
                    dst_ref=other.at[hop - 1, field, pl.ds(start, count)],
                    send_sem=state_send.at[hop - 1, number],
                    recv_sem=state_recv.at[hop - 1, number],
                    device_id=(slab, lax.rem(half + hop, halves)),
                    device_id_type=MESH,
                )
            )
        for copy in copies:
            copy.start()
        pieces.append((field, start, count, copies))

    def inner_speed(group, carry):
        at = pl.ds(pl.multiple_of(group * 8, 8), 8)
        mask = mushy[2 : depth + 2]
        speed = advance_speed(raw[SPEED, 2 : depth + 2, at, :], mask)
        own[SPEED, 2 : depth - 2, at, :] = advance_speed(speed, mask[1:-1])
        return carry

    lax.fori_loop(0, groups, inner_speed, 0)
    middle = depth // 2
    send(SPEED, 2, middle - 2)
    send(SPEED, middle, middle - 2)

    def inner_pair(group, carry):
        at = pl.ds(pl.multiple_of(group * 8, 8), 8)
        mask = mushy[2 : depth + 2]
        before = raw[SPEED, 2 : depth + 2, at, :]
        heat, solute = advance_pair(
            raw[HEAT, 2 : depth + 2, at, :], raw[SOLUTE, 2 : depth + 2, at, :], before, mask
        )
        heat, solute = advance_pair(heat, solute, advance_speed(before, mask), mask[1:-1])
        own[HEAT, 2 : depth - 2, at, :] = heat
        own[SOLUTE, 2 : depth - 2, at, :] = solute
        return carry

    lax.fori_loop(0, groups, inner_pair, 0)
    send(HEAT, 2, middle - 2)
    send(HEAT, middle, middle - 2)

    @pl.when(jnp.logical_not(last))
    def _():
        for copy in up:
            copy.wait_recv()

    @pl.when(jnp.logical_not(first))
    def _():
        for copy in down:
            copy.wait_recv()

    def edges(group, carry):
        at = pl.ds(pl.multiple_of(group * 8, 8), 8)
        for begin, outside, edge in ((0, first, 0), (depth - 2, last, 3)):
            mask = mushy[begin : begin + 6]
            before = raw[SPEED, begin : begin + 6, at, :]
            heat, solute = advance_pair(
                raw[HEAT, begin : begin + 6, at, :], raw[SOLUTE, begin : begin + 6, at, :], before, mask
            )
            speed = advance_speed(before, mask)
            row = lax.broadcasted_iota(jnp.int32, heat.shape, 0)
            beyond = jnp.logical_and(row == edge, outside)
            heat, solute, speed = [jnp.where(beyond, 0.0, q) for q in (heat, solute, speed)]
            mask = mask[1:-1]
            new_heat, new_solute = advance_pair(heat, solute, speed, mask)
            own[HEAT, begin : begin + 2, at, :] = new_heat
            own[SOLUTE, begin : begin + 2, at, :] = new_solute
            own[SPEED, begin : begin + 2, at, :] = advance_speed(speed, mask)
        return carry

    lax.fori_loop(0, groups, edges, 0)

    lane = lax.broadcasted_iota(jnp.int32, (members, width), 1)
    per_slab = index_ref.shape[0]
    observed = jnp.zeros((members, width), jnp.float32)
    value = jnp.zeros((members, width), jnp.float32)
    error = jnp.ones((members, width), jnp.float32)
    for o in range(per_slab):
        cell = index_ref[o]
        z = cell // width
        w = cell - z * width
        factor = 1.0 - mushy[z + 2][0:1] * (1.0 - mushy_ratio)
        temp = jnp.where(lane == w, own[HEAT, z] * factor, 0.0)
        observed = jnp.where(lane == o, jnp.sum(temp, axis=1, keepdims=True), observed)
        value = jnp.where(lane == o, value_ref[o], value)
        error = jnp.where(lane == o, error_ref[o], error)
    square[...] = jnp.zeros((ens, width), jnp.float32)
    square[pl.ds(pl.multiple_of(half * members, 8), members), :] = (observed - value) / error
    turned = square[...].T
    seen[me] = turned[0:8] + pltpu.roll(turned[8:16], ens // 2, 1)

    def tell_copy(peer):
        return pltpu.make_async_remote_copy(
            src_ref=seen.at[me],
            dst_ref=seen.at[me],
            send_sem=seen_send.at[0],
            recv_sem=seen_recv.at[0],
            device_id=(peer // halves, lax.rem(peer, halves)),
            device_id_type=MESH,
        )

    def tell(step, carry):
        tell_copy(lax.rem(me + step, everyone)).start()
        return carry

    lax.fori_loop(1, everyone, tell, 0)

    for field in range(3):
        send(field, 0, 2)
        send(field, depth - 2, 2)
    send(SOLUTE, 2, middle - 2)
    send(SOLUTE, middle, middle - 2)

    rest = seen.at[pl.ds(0, everyone - 1)]
    pltpu.make_async_copy(rest, rest, seen_recv.at[0]).wait()

    got = seen[...].reshape(slabs, halves, 8, ens)
    place = lax.broadcasted_iota(jnp.int32, (slabs, 8, ens), 2)
    low = jnp.zeros((slabs, 8, ens), jnp.float32)
    high = jnp.zeros((slabs, 8, ens), jnp.float32)
    for m in range(halves):
        mine = (place >= m * members) & (place < (m + 1) * members)
        low = jnp.where(mine, got[:, m], low)
        high = jnp.where(mine, pltpu.roll(got[:, m], ens // 2, 2), high)
    deviation = jnp.concatenate(
        [low.reshape(slabs * 8, ens), high.reshape(slabs * 8, ens)], axis=0
    )
    mean = jnp.sum(deviation, axis=1, keepdims=True) * (1.0 / ens)
    root = 1.0 / (ens - 1.0) ** 0.5
    spread = (deviation - mean) * root
    project = -jnp.sum(spread * mean, axis=0, keepdims=True)
    gram = lax.dot_general(
        spread, spread, (((0,), (0,)), ((), ())),
        precision=HIGHEST, preferred_element_type=jnp.float32,
    )
    rows = lax.broadcasted_iota(jnp.int32, (ens, ens), 0)
    lanes = lax.broadcasted_iota(jnp.int32, (ens, ens), 1)
    square[...] = jnp.where(rows == lanes, 1.0, 0.0) + gram
    inverse_factor(square)
    inverse = square[...]
    shift = jnp.sum(inverse * project, axis=1, keepdims=True)
    shift = jnp.sum(inverse * shift, axis=0, keepdims=True)
    combined = inverse + shift * root
    combined = combined - jnp.sum(combined, axis=1, keepdims=True) * (1.0 / ens) + 1.0 / ens
    square[...] = pltpu.roll(combined, lax.rem(ens - half * members, ens), 1)
    weight_high, weight_low = split(square[pl.ds(pl.multiple_of(half * members, 8), members), :])
    weights = jnp.concatenate([weight_high, weight_high, weight_low], axis=1)

    for field, start, count, copies in pieces:
        for copy in copies:
            copy.wait_recv()
        for z in range(start, start + count, 2):
            parts = []
            for d in (z, z + 1):
                blocks = [own[field, d]] + [
                    other[halves - q - 1, field, d] for q in range(1, halves)
                ]
                parts.append(jnp.concatenate(blocks, axis=0))
            state_high, state_low = split(jnp.concatenate(parts, axis=1))
            mixed = jnp.dot(
                weights,
                jnp.concatenate([state_high, state_low, state_high], axis=0),
                preferred_element_type=jnp.float32,
            )
            for i, d in enumerate((z, z + 1)):
                block = mixed[:, i * width : (i + 1) * width]
                if field == SPEED:
                    vel[pl.ds(d, members, stride=depth), :] = block
                else:
                    hc[pl.ds(field * depth + d, members, stride=2 * depth), :] = block

    store_v = pltpu.make_async_copy(vel, out_v_ref, out_sem.at[0])
    store_hc = pltpu.make_async_copy(hc, out_hc_ref, out_sem.at[1])
    store_v.start()
    store_hc.start()

    for _, _, _, copies in pieces:
        for copy in copies:
            copy.wait_send()
    pltpu.make_async_copy(rest, rest, seen_send.at[0]).wait()

    @pl.when(jnp.logical_not(first))
    def _():
        for copy in up:
            copy.wait_send()

    @pl.when(jnp.logical_not(last))
    def _():
        for copy in down:
            copy.wait_send()

    store_v.wait()
    store_hc.wait()


def on_device(slabs, halves, member_heat_solute, velocity, phase_mask, obs_index, obs_value, obs_error):
    members, _, depth, width = member_heat_solute.shape
    ens = members * halves
    vmem = pl.BlockSpec(memory_space=pltpu.VMEM)
    smem = pl.BlockSpec(memory_space=pltpu.SMEM)
    anywhere = pl.BlockSpec(memory_space=pl.ANY)
    hc, vel = pl.pallas_call(
        functools.partial(kernel, slabs, halves),
        out_shape=(
            jax.ShapeDtypeStruct((members * 2 * depth, width), jnp.float32),
            jax.ShapeDtypeStruct((members * depth, width), jnp.float32),
        ),
        in_specs=[anywhere, anywhere, vmem, smem, smem, smem],
        out_specs=(anywhere, anywhere),
        scratch_shapes=[
            pltpu.VMEM((members * 2 * depth, width), jnp.float32),
            pltpu.VMEM((members * depth, width), jnp.float32),
            pltpu.VMEM((3, depth + 4, members, width), jnp.float32),
            pltpu.VMEM((depth + 4, 8, width), jnp.float32),
            pltpu.VMEM((3, depth, members, width), jnp.float32),
            pltpu.VMEM((halves - 1, 3, depth, members, width), jnp.float32),
            pltpu.VMEM((slabs * halves, 8, ens), jnp.float32),
            pltpu.VMEM((ens, ens), jnp.float32),
            pltpu.SemaphoreType.DMA((2,)),
            pltpu.SemaphoreType.DMA((2,)),
            pltpu.SemaphoreType.DMA((2, 2)),
            pltpu.SemaphoreType.DMA((2, 2)),
            pltpu.SemaphoreType.DMA((halves - 1, 12)),
            pltpu.SemaphoreType.DMA((halves - 1, 12)),
            pltpu.SemaphoreType.DMA((1,)),
            pltpu.SemaphoreType.DMA((1,)),
        ],
        compiler_params=pltpu.CompilerParams(
            collective_id=0, has_side_effects=True, vmem_limit_bytes=48 * 1024 * 1024
        ),
    )(
        member_heat_solute.reshape(-1, width),
        velocity.reshape(-1, width),
        phase_mask,
        obs_index,
        obs_value,
        obs_error,
    )
    return hc.reshape(members, 2, depth, width), vel.reshape(members, depth, width)


def solution(mesh):
    return jax.shard_map(
        functools.partial(on_device, mesh.shape["space"], mesh.shape["mem"]),
        mesh=mesh,
        in_specs=(
            P("mem", None, "space", None),
            P("mem", "space", None),
            P("space", None),
            P("space"),
            P("space"),
            P("space"),
        ),
        out_specs=(P("mem", None, "space", None), P("mem", "space", None)),
        check_vma=False,
    )
```

time: 593 us -> 53.6 us (0.09)
  matrix products: 213 us -> 0 us
  loops' own time: 95.3 us -> 0 us
  other arithmetic: 87 us -> 0 us
  local copies, waits for them, and re-layouts: 72.6 us -> 5.39 us
  waiting for transfers between devices: 58.8 us -> 0 us
  Pallas kernels: 0 us -> 47.3 us
  blocking collectives: 36.6 us -> 0 us
  between operations: 15.8 us -> 0.67 us
  starting transfers between devices: 10.5 us -> 0 us
    dot_general x263 -> x0, matrix products: 213 us -> none  [the longest x128 105 us: column(): jnp.dot(lower, lower_row, precision=lax.Precision.HIGHEST)]
    another operation x2 -> x0, loops' own time: 95.3 us -> none  [the longest x1 92.6 us: factorize(): lax.fori_loop(0, order, column, jnp.zeros((order, order), jnp.float32))]
    reduce_sum x129 -> x0, other arithmetic: 77.7 us -> none  [the longest x128 77.6 us: row_step(): pivot = jnp.sum(jnp.where(positions == i, lower_row, 0.0))]
    psum x1 -> x0, waiting for transfers between devices: 52.7 us -> none  [on_device(): gram, project = lax.psum((local_gram, local_project), 'space')]
    dynamic_update_slice x256 -> x0, local copies, waits for them, and re-layouts: 49.9 us -> none  [the longest x128 45.9 us: column(): return lax.dynamic_update_slice(lower, new_col[:, None], (jnp.int32(0), j))]
    pallas_call x0 -> x1, Pallas kernels: none -> 47.3 us  [on_device(): pl.pallas_call(functools.partial(kernel, slabs, halves), out_shape=(jax.S...]
    psum x1 -> x0, blocking collectives: 32.2 us -> none  [on_device(): gram, project = lax.psum((local_gram, local_project), 'space')]
    broadcast_in_dim x128 -> x0, local copies, waits for them, and re-layouts: 14.5 us -> none  [column(): return lax.dynamic_update_slice(lower, new_col[:, None], (jnp.int32(0), j))]
  transfers between devices with their start and end apart: 6 -> 0, of which waited for: 3 -> 0; matrix products, arithmetic and copies ran while one was open for 60% -> 0% of each run, Pallas kernels for 0% -> 0%
where the time goes in v1:
time: 53.6 us; the launch traced here: 53.4 us
  Pallas kernels  47.3 us (88%)
  local copies, waits for them, and re-layouts  5.39 us (10%)
  between operations  0.67 us (1%)
    pallas_call x1, Pallas kernels, on_device(): pl.pallas_call(functools.partial(kernel, slabs, halves), out_shape=(jax.S...  47.3 us
    unnamed x14, local copies, waits for them, and re-layouts  5.39 us

profile of v1, /device:TPU:0, one launch (start us, length us, event | category | flops | bytes accessed | tf_op | source)
XLA Modules:
  0.0 53.4 jit_solution(18211782395020589266)
XLA Ops:
  0.6 0.0 copy-start.3
  0.6 0.0 copy-start.4
  0.7 0.0 copy-start.5
  0.7 0.6 %copy-done.3 = s32[16]{0:T(128)S(1)} copy-done((s32[16]{0:T(128)S(1)}, s32[16]{0:T(128)}, u32[]{:S(2)}) %copy-start.3) | copy-done | bytes 88
  1.3 0.0 copy-done.4
  1.3 0.0 copy-done.5
  1.3 0.0 copy-start
  1.3 1.2 %copy-done = f32[64,2,16,128]{3,2,1,0:T(8,128)S(1)} copy-done((f32[64,2,16,128]{3,2,1,0:T(8,128)S(1)}, f32[64,2,16,128]{3,2,1,0:T(8,128)}, u32[]{:S(2)}) %copy-start) | copy-done | bytes 1048600
  2.5 0.0 copy-start.1
  2.5 1.0 %copy-done.1 = f32[64,16,128]{2,1,0:T(8,128)S(1)} copy-done((f32[64,16,128]{2,1,0:T(8,128)S(1)}, f32[64,16,128]{2,1,0:T(8,128)}, u32[]{:S(2)}) %copy-start.1) | copy-done | bytes 524312
  3.6 0.0 copy-start.2
  3.6 0.7 %copy-done.2 = s32[16,128]{1,0:T(8,128)S(1)} copy-done((s32[16,128]{1,0:T(8,128)S(1)}, s32[16,128]{1,0:T(8,128)}, u32[]{:S(2)}) %copy-start.2) | copy-done | bytes 8216
  4.3 47.3 %shard_map.77 = (f32[2048,128]{1,0:T(8,128)S(1)}, f32[1024,128]{1,0:T(8,128)S(1)}) custom-call(f32[2048,128]{1,0:T(8,128)S(1)} %bitcast.4, f32[1024,128]{1,0:T(8,128)S(1)} %bitcast.6, s32[16,128]{1,0:T(8,128)S(1)} %copy-done.2, s32[16]{0:T(128)S(1)} %copy-done.3, f32[16]{0:T(128)S(1)} %copy-done.4, f32[16]{0:T(128)S(1)} %copy-done.5), custom_call_target="tpu_custom_call" | custom-call | tf_op jit(solution)/shard_map/pallas_call | solution.py:404
  51.6 1.0 %copy.10 = f32[64,2,16,128]{3,2,1,0:T(8,128)} copy(f32[64,2,16,128]{3,2,1,0:T(8,128)S(1)} %bitcast.5) | data formatting | bytes 2097152
  52.6 0.8 %copy.11 = f32[64,16,128]{2,1,0:T(8,128)} copy(f32[64,16,128]{2,1,0:T(8,128)S(1)} %bitcast.7) | data formatting | bytes 1048576
Async XLA Ops:
  0.6 0.7 %copy-start.3 = (s32[16]{0:T(128)S(1)}, s32[16]{0:T(128)}, u32[]{:S(2)}) copy-start(s32[16]{0:T(128)} %index_ref.1) | copy-start | bytes 196
  0.6 0.7 %copy-start.4 = (f32[16]{0:T(128)S(1)}, f32[16]{0:T(128)}, u32[]{:S(2)}) copy-start(f32[16]{0:T(128)} %value_ref.1) | copy-start | bytes 196
  0.7 0.7 %copy-start.5 = (f32[16]{0:T(128)S(1)}, f32[16]{0:T(128)}, u32[]{:S(2)}) copy-start(f32[16]{0:T(128)} %error_ref.1) | copy-start | bytes 196
  1.3 1.2 %copy-start = (f32[64,2,16,128]{3,2,1,0:T(8,128)S(1)}, f32[64,2,16,128]{3,2,1,0:T(8,128)}, u32[]{:S(2)}) copy-start(f32[64,2,16,128]{3,2,1,0:T(8,128)} %param.6) | copy-start | bytes 3145732
  2.5 1.0 %copy-start.1 = (f32[64,16,128]{2,1,0:T(8,128)S(1)}, f32[64,16,128]{2,1,0:T(8,128)}, u32[]{:S(2)}) copy-start(f32[64,16,128]{2,1,0:T(8,128)} %param.7) | copy-start | bytes 1572868
  3.6 0.7 %copy-start.2 = (s32[16,128]{1,0:T(8,128)S(1)}, s32[16,128]{1,0:T(8,128)}, u32[]{:S(2)}) copy-start(s32[16,128]{1,0:T(8,128)} %mask_ref.1) | copy-start | bytes 24580

commit v2 on v1

--- a/solution.py
+++ b/solution.py
@@ -107,9 +107,9 @@
 
 def kernel(
     slabs, halves,
-    hc_ref, v_ref, mask_ref, index_ref, value_ref, error_ref,
+    hc_ref, v_ref, phase_ref, cell_ref, datum_ref, deviate_ref,
     out_hc_ref, out_v_ref,
-    hc, vel, raw, mushy, own, other, seen, square,
+    mask_ref, index_ref, value_ref, error_ref, hc, vel, raw, mushy, own, other, seen, square,
     in_sem, out_sem, halo_send, halo_recv, state_send, state_recv, seen_send, seen_recv,
 ):
     members = own.shape[2]
@@ -126,8 +126,17 @@
 
     load_v = pltpu.make_async_copy(v_ref, vel, in_sem.at[0])
     load_hc = pltpu.make_async_copy(hc_ref, hc, in_sem.at[1])
+    load_mask = pltpu.make_async_copy(phase_ref, mask_ref, in_sem.at[2])
+    load_observed = [
+        pltpu.make_async_copy(cell_ref, index_ref, in_sem.at[3]),
+        pltpu.make_async_copy(datum_ref, value_ref, in_sem.at[4]),
+        pltpu.make_async_copy(deviate_ref, error_ref, in_sem.at[5]),
+    ]
+    load_mask.start()
     load_v.start()
     load_hc.start()
+    for load in load_observed:
+        load.start()
 
     barrier = pltpu.get_barrier_semaphore()
 
@@ -140,19 +149,33 @@
 
     lax.fori_loop(1, everyone, greet, 0)
 
+    load_mask.wait()
     for z in range(depth):
         row = mask_ref[z : z + 1, :].astype(jnp.float32)
         mushy[z + 2] = jnp.broadcast_to(row, (8, width))
 
-    def relayout(zs):
+    def relayout_speed(zs):
+        for z in zs:
+            raw[SPEED, z + 2] = vel[pl.ds(z, members, stride=depth), :]
+
+    def relayout_pair(zs):
         for z in zs:
             raw[HEAT, z + 2] = hc[pl.ds(z, members, stride=2 * depth), :]
             raw[SOLUTE, z + 2] = hc[pl.ds(depth + z, members, stride=2 * depth), :]
-            raw[SPEED, z + 2] = vel[pl.ds(z, members, stride=depth), :]
 
     load_v.wait()
+    relayout_speed(range(depth))
+
+    def inner_speed(group, carry):
+        at = pl.ds(pl.multiple_of(group * 8, 8), 8)
+        mask = mushy[2 : depth + 2]
+        speed = advance_speed(raw[SPEED, 2 : depth + 2, at, :], mask)
+        own[SPEED, 2 : depth - 2, at, :] = advance_speed(speed, mask[1:-1])
+        return carry
+
+    lax.fori_loop(0, groups, inner_speed, 0)
     load_hc.wait()
-    relayout((0, 1, depth - 2, depth - 1))
+    relayout_pair((0, 1, depth - 2, depth - 1))
 
     def halo(direction, source, target, to, part):
         ref = raw if part == 0 else mushy
@@ -190,8 +213,6 @@
     def _():
         for copy in down:
             copy.start()
-
-    relayout(range(2, depth - 2))
 
     pieces = []
 
@@ -213,17 +234,10 @@
             copy.start()
         pieces.append((field, start, count, copies))
 
-    def inner_speed(group, carry):
-        at = pl.ds(pl.multiple_of(group * 8, 8), 8)
-        mask = mushy[2 : depth + 2]
-        speed = advance_speed(raw[SPEED, 2 : depth + 2, at, :], mask)
-        own[SPEED, 2 : depth - 2, at, :] = advance_speed(speed, mask[1:-1])
-        return carry
-
-    lax.fori_loop(0, groups, inner_speed, 0)
     middle = depth // 2
     send(SPEED, 2, middle - 2)
     send(SPEED, middle, middle - 2)
+    relayout_pair(range(2, depth - 2))
 
     def inner_pair(group, carry):
         at = pl.ds(pl.multiple_of(group * 8, 8), 8)
@@ -238,8 +252,6 @@
         return carry
 
     lax.fori_loop(0, groups, inner_pair, 0)
-    send(HEAT, 2, middle - 2)
-    send(HEAT, middle, middle - 2)
 
     @pl.when(jnp.logical_not(last))
     def _():
@@ -274,6 +286,8 @@
 
     lane = lax.broadcasted_iota(jnp.int32, (members, width), 1)
     per_slab = index_ref.shape[0]
+    for load in load_observed:
+        load.wait()
     observed = jnp.zeros((members, width), jnp.float32)
     value = jnp.zeros((members, width), jnp.float32)
     error = jnp.ones((members, width), jnp.float32)
@@ -307,11 +321,12 @@
 
     lax.fori_loop(1, everyone, tell, 0)
 
-    for field in range(3):
+    for field in (SPEED, HEAT, SOLUTE):
         send(field, 0, 2)
         send(field, depth - 2, 2)
-    send(SOLUTE, 2, middle - 2)
-    send(SOLUTE, middle, middle - 2)
+        if field != SPEED:
+            send(field, 2, middle - 2)
+            send(field, middle, middle - 2)
 
     rest = seen.at[pl.ds(0, everyone - 1)]
     pltpu.make_async_copy(rest, rest, seen_recv.at[0]).wait()
@@ -348,7 +363,11 @@
     weight_high, weight_low = split(square[pl.ds(pl.multiple_of(half * members, 8), members), :])
     weights = jnp.concatenate([weight_high, weight_high, weight_low], axis=1)
 
+    store_v = pltpu.make_async_copy(vel, out_v_ref, out_sem.at[0])
+    store_hc = pltpu.make_async_copy(hc, out_hc_ref, out_sem.at[1])
     for field, start, count, copies in pieces:
+        if field == HEAT and start == 0:
+            store_v.start()
         for copy in copies:
             copy.wait_recv()
         for z in range(start, start + count, 2):
@@ -371,9 +390,6 @@
                 else:
                     hc[pl.ds(field * depth + d, members, stride=2 * depth), :] = block
 
-    store_v = pltpu.make_async_copy(vel, out_v_ref, out_sem.at[0])
-    store_hc = pltpu.make_async_copy(hc, out_hc_ref, out_sem.at[1])
-    store_v.start()
     store_hc.start()
 
     for _, _, _, copies in pieces:
@@ -398,18 +414,20 @@
 def on_device(slabs, halves, member_heat_solute, velocity, phase_mask, obs_index, obs_value, obs_error):
     members, _, depth, width = member_heat_solute.shape
     ens = members * halves
-    vmem = pl.BlockSpec(memory_space=pltpu.VMEM)
-    smem = pl.BlockSpec(memory_space=pltpu.SMEM)
-    anywhere = pl.BlockSpec(memory_space=pl.ANY)
+    anywhere = pl.BlockSpec(memory_space=pltpu.HBM)
     hc, vel = pl.pallas_call(
         functools.partial(kernel, slabs, halves),
         out_shape=(
             jax.ShapeDtypeStruct((members * 2 * depth, width), jnp.float32),
             jax.ShapeDtypeStruct((members * depth, width), jnp.float32),
         ),
-        in_specs=[anywhere, anywhere, vmem, smem, smem, smem],
+        in_specs=[anywhere] * 6,
         out_specs=(anywhere, anywhere),
         scratch_shapes=[
+            pltpu.VMEM((depth, width), jnp.int32),
+            pltpu.SMEM(obs_index.shape, jnp.int32),
+            pltpu.SMEM(obs_value.shape, jnp.float32),
+            pltpu.SMEM(obs_error.shape, jnp.float32),
             pltpu.VMEM((members * 2 * depth, width), jnp.float32),
             pltpu.VMEM((members * depth, width), jnp.float32),
             pltpu.VMEM((3, depth + 4, members, width), jnp.float32),
@@ -418,7 +436,7 @@
             pltpu.VMEM((halves - 1, 3, depth, members, width), jnp.float32),
             pltpu.VMEM((slabs * halves, 8, ens), jnp.float32),
             pltpu.VMEM((ens, ens), jnp.float32),
-            pltpu.SemaphoreType.DMA((2,)),
+            pltpu.SemaphoreType.DMA((6,)),
             pltpu.SemaphoreType.DMA((2,)),
             pltpu.SemaphoreType.DMA((2, 2)),
             pltpu.SemaphoreType.DMA((2, 2)),
@@ -428,7 +446,7 @@
             pltpu.SemaphoreType.DMA((1,)),
         ],
         compiler_params=pltpu.CompilerParams(
-            collective_id=0, has_side_effects=True, vmem_limit_bytes=48 * 1024 * 1024
+            collective_id=0, has_side_effects=True, vmem_limit_bytes=62 * 1024 * 1024
         ),
     )(
         member_heat_solute.reshape(-1, width),

time: 53.6 us -> 49.4 us (0.922)
  local copies, waits for them, and re-layouts: 5.39 us -> 3.12 us
  Pallas kernels: 47.3 us -> 45.4 us
    unnamed x14 -> x4, local copies, waits for them, and re-layouts: 5.39 us -> 3.12 us
    pallas_call x1, Pallas kernels: 47.3 us -> 45.4 us  [on_device(): pl.pallas_call(functools.partial(kernel, slabs, halves), out_shape=(jax.S...]
where the time goes in v2:
time: 49.4 us; the launch traced here: 49.1 us
  Pallas kernels  45.4 us (92%)
  local copies, waits for them, and re-layouts  3.12 us (6%)
  between operations  0.65 us (1%)
    pallas_call x1, Pallas kernels, on_device(): pl.pallas_call(functools.partial(kernel, slabs, halves), out_shape=(jax.S...  45.4 us
    unnamed x4, local copies, waits for them, and re-layouts  3.12 us

profile of v2, /device:TPU:0, one launch (start us, length us, event | category | flops | bytes accessed | tf_op | source)
XLA Modules:
  0.0 49.1 jit_solution(16443182950576317713)
XLA Ops:
  0.6 45.4 %shard_map.77 = (f32[2048,128]{1,0:T(8,128)}, f32[1024,128]{1,0:T(8,128)}) custom-call(f32[2048,128]{1,0:T(8,128)} %bitcast.4, f32[1024,128]{1,0:T(8,128)} %bitcast.6, s32[16,128]{1,0:T(8,128)} %phase_ref.1, s32[16]{0:T(128)} %cell_ref.1, f32[16]{0:T(128)} %datum_ref.1, f32[16]{0:T(128)} %deviate_ref.1), custom_call_target="tpu_custom_call" | custom-call | tf_op jit(solution)/shard_map/pallas_call | solution.py:418
  46.0 0.0 copy-start
  46.0 2.3 %copy.10 = f32[64,2,16,128]{3,2,1,0:T(8,128)} copy(f32[64,2,16,128]{3,2,1,0:T(8,128)} %bitcast.5) | data formatting | bytes 2097152
  48.3 0.0 copy-done
  48.4 0.8 %copy.11 = f32[64,16,128]{2,1,0:T(8,128)} copy(f32[64,16,128]{2,1,0:T(8,128)S(1)} %bitcast.7) | data formatting | bytes 1048576
Async XLA Ops:
  46.0 2.3 %copy-start = (f32[1024,128]{1,0:T(8,128)S(1)}, f32[1024,128]{1,0:T(8,128)}, u32[]{:S(2)}) copy-start(f32[1024,128]{1,0:T(8,128)} %get-tuple-element.5) | copy-start | bytes 1572868

commit v3 on v2

--- a/solution.py
+++ b/solution.py
@@ -18,7 +18,7 @@
 MESH = pl.DeviceIdType.MESH
 HIGHEST = lax.Precision.HIGHEST
 HEAT, SOLUTE, SPEED = 0, 1, 2
-PANEL = 8
+PANEL = 16
 
 
 def lateral_sum(field):
@@ -58,6 +58,15 @@
     high = values.astype(jnp.bfloat16)
     low = (values - high.astype(jnp.float32)).astype(jnp.bfloat16)
     return high, low
+
+
+def split_three(values):
+    parts = []
+    for _ in range(3):
+        part = values.astype(jnp.bfloat16).astype(jnp.float32)
+        parts.append(part)
+        values = values - part
+    return parts
 
 
 def inverse_factor(matrix_ref):
@@ -92,9 +101,13 @@
         upper = upper * scale
         inverse = inverse * scale
         right = jnp.where(lane < base + PANEL, inverse, upper)
+        upper_parts = split_three(upper)
+        right_parts = split_three(right)
         change = lax.dot_general(
-            upper, right, (((0,), (0,)), ((), ())),
-            precision=HIGHEST, preferred_element_type=jnp.float32,
+            jnp.concatenate([upper_parts[i] for i in (0, 0, 1, 1, 0, 2)], axis=0).astype(jnp.bfloat16),
+            jnp.concatenate([right_parts[i] for i in (0, 1, 0, 1, 2, 0)], axis=0).astype(jnp.bfloat16),
+            (((0,), (0,)), ((), ())),
+            preferred_element_type=jnp.float32,
         )
         old = matrix_ref[...]
         kept = jnp.where((lanes >= base) & (lanes < base + PANEL), 0.0, old)
@@ -110,7 +123,7 @@
     hc_ref, v_ref, phase_ref, cell_ref, datum_ref, deviate_ref,
     out_hc_ref, out_v_ref,
     mask_ref, index_ref, value_ref, error_ref, hc, vel, raw, mushy, own, other, seen, square,
-    in_sem, out_sem, halo_send, halo_recv, state_send, state_recv, seen_send, seen_recv,
+    in_sem, halo_send, halo_recv, state_send, state_recv, seen_send, seen_recv,
 ):
     members = own.shape[2]
     width = own.shape[3]
@@ -363,11 +376,7 @@
     weight_high, weight_low = split(square[pl.ds(pl.multiple_of(half * members, 8), members), :])
     weights = jnp.concatenate([weight_high, weight_high, weight_low], axis=1)
 
-    store_v = pltpu.make_async_copy(vel, out_v_ref, out_sem.at[0])
-    store_hc = pltpu.make_async_copy(hc, out_hc_ref, out_sem.at[1])
     for field, start, count, copies in pieces:
-        if field == HEAT and start == 0:
-            store_v.start()
         for copy in copies:
             copy.wait_recv()
         for z in range(start, start + count, 2):
@@ -386,11 +395,9 @@
             for i, d in enumerate((z, z + 1)):
                 block = mixed[:, i * width : (i + 1) * width]
                 if field == SPEED:
-                    vel[pl.ds(d, members, stride=depth), :] = block
+                    out_v_ref[pl.ds(d, members, stride=depth), :] = block
                 else:
-                    hc[pl.ds(field * depth + d, members, stride=2 * depth), :] = block
-
-    store_hc.start()
+                    out_hc_ref[pl.ds(field * depth + d, members, stride=2 * depth), :] = block
 
     for _, _, _, copies in pieces:
         for copy in copies:
@@ -407,22 +414,20 @@
         for copy in down:
             copy.wait_send()
 
-    store_v.wait()
-    store_hc.wait()
-
 
 def on_device(slabs, halves, member_heat_solute, velocity, phase_mask, obs_index, obs_value, obs_error):
     members, _, depth, width = member_heat_solute.shape
     ens = members * halves
+    held = pl.BlockSpec(memory_space=pltpu.VMEM)
     anywhere = pl.BlockSpec(memory_space=pltpu.HBM)
     hc, vel = pl.pallas_call(
         functools.partial(kernel, slabs, halves),
         out_shape=(
-            jax.ShapeDtypeStruct((members * 2 * depth, width), jnp.float32),
-            jax.ShapeDtypeStruct((members * depth, width), jnp.float32),
+            pltpu.VMEM((members * 2 * depth, width), jnp.float32),
+            pltpu.VMEM((members * depth, width), jnp.float32),
         ),
         in_specs=[anywhere] * 6,
-        out_specs=(anywhere, anywhere),
+        out_specs=(held, held),
         scratch_shapes=[
             pltpu.VMEM((depth, width), jnp.int32),
             pltpu.SMEM(obs_index.shape, jnp.int32),
@@ -437,7 +442,6 @@
             pltpu.VMEM((slabs * halves, 8, ens), jnp.float32),
             pltpu.VMEM((ens, ens), jnp.float32),
             pltpu.SemaphoreType.DMA((6,)),
-            pltpu.SemaphoreType.DMA((2,)),
             pltpu.SemaphoreType.DMA((2, 2)),
             pltpu.SemaphoreType.DMA((2, 2)),
             pltpu.SemaphoreType.DMA((halves - 1, 12)),
@@ -446,15 +450,20 @@
             pltpu.SemaphoreType.DMA((1,)),
         ],
         compiler_params=pltpu.CompilerParams(
-            collective_id=0, has_side_effects=True, vmem_limit_bytes=62 * 1024 * 1024
+            collective_id=0, has_side_effects=True, vmem_limit_bytes=40 * 1024 * 1024
         ),
     )(
-        member_heat_solute.reshape(-1, width),
-        velocity.reshape(-1, width),
-        phase_mask,
-        obs_index,
-        obs_value,
-        obs_error,
+        *[
+            pltpu.with_memory_space_constraint(x, pltpu.HBM)
+            for x in (
+                member_heat_solute.reshape(-1, width),
+                velocity.reshape(-1, width),
+                phase_mask,
+                obs_index,
+                obs_value,
+                obs_error,
+            )
+        ]
     )
     return hc.reshape(members, 2, depth, width), vel.reshape(members, depth, width)
 

time: 49.4 us -> 47 us (0.951)
  local copies, waits for them, and re-layouts: 3.12 us -> 1.77 us
  Pallas kernels: 45.4 us -> 44.4 us
    unnamed x4 -> x2, local copies, waits for them, and re-layouts: 3.12 us -> 1.77 us
    pallas_call x1, Pallas kernels: 45.4 us -> 44.4 us  [on_device(): pl.pallas_call(functools.partial(kernel, slabs, halves), out_shape=(pltpu...]
where the time goes in v3:
time: 47 us; the launch traced here: 46.8 us
  Pallas kernels  44.4 us (94%)
  local copies, waits for them, and re-layouts  1.77 us (4%)
  between operations  0.64 us (1%)
    pallas_call x1, Pallas kernels, on_device(): pl.pallas_call(functools.partial(kernel, slabs, halves), out_shape=(pltpu...  44.4 us
    unnamed x2, local copies, waits for them, and re-layouts  1.77 us

profile of v3, /device:TPU:0, one launch (start us, length us, event | category | flops | bytes accessed | tf_op | source)
XLA Modules:
  0.0 46.8 jit_solution(5477409006053901906)
XLA Ops:
  0.6 44.4 %shard_map.77 = (f32[2048,128]{1,0:T(8,128)S(1)}, f32[1024,128]{1,0:T(8,128)S(1)}) custom-call(f32[2048,128]{1,0:T(8,128)} %bitcast.6, f32[1024,128]{1,0:T(8,128)} %bitcast.7, s32[16,128]{1,0:T(8,128)} %phase_ref.1, s32[16]{0:T(128)} %cell_ref.1, f32[16]{0:T(128)} %datum_ref.1, f32[16]{0:T(128)} %deviate_ref.1), custom_call_target="tpu_custom_call" | custom-call | tf_op jit(solution)/shard_map/pallas_call | solution.py:423
  45.0 1.0 %copy.10 = f32[64,2,16,128]{3,2,1,0:T(8,128)} copy(f32[64,2,16,128]{3,2,1,0:T(8,128)S(1)} %bitcast.4) | data formatting | bytes 2097152
  46.0 0.8 %copy.11 = f32[64,16,128]{2,1,0:T(8,128)} copy(f32[64,16,128]{2,1,0:T(8,128)S(1)} %bitcast.5) | data formatting | bytes 1048576
